TPU v7x, 1024 devices: a whole 4x4x32 slice. The times are simulated.
1024 devices in a mesh: sub: 64 (over z, core), dom: 16 (over x, y).
Axes of the slice: x: 4, y: 4, z: 32, core: 2. Of those that a mesh axis runs over, the one named last changes fastest.
Arguments:
- a_cols: int32 [3072, 27], P(('sub', 'dom')), may hold values from 0 to 24, as said below
- a_blocks: bfloat16 [3072, 27, 128, 128], P(('sub', 'dom')), may hold values from -0.5 to 0.5
- p_blocks: bfloat16 [3072, 128, 128], P(('sub', 'dom')), may hold values from -1.1953125 to 1.1953125
- send_rows: int32 [16384, 1], P(('sub', 'dom')), may hold values from -1 to 2, as said below
Outputs:
- coarse: bfloat16 [1024, 128, 2304], P(('sub', 'dom'))
Inputs may be any that keep to these rules, and one draw needn't show every extreme that they name: a_cols[i, 0] is 3 + i % 3 (the row itself). Codes below 3 occur only for subdomains s > 0, codes from 6 to 8 only for s < 63. A code 3 * 3 + p + m has p != d and names a slot m that holds a row in the list of device (s, p) to device (s, d). Codes may repeat within a row; repeated blocks add. `send_rows`: entry (s * 16 + p) * 16 + d lists distinct rows of device (s, p) for device (s, d), then -1; the list of a device to itself is all -1. Every listed row is named by some code of the receiving device. In every draw and every subdomain some pair holds 1 row; the number per pair is uneven, some receivers get 1 from every peer.
All inputs are finite; a program needn't handle non-finite values.
Results may differ from a plain program's by a relative error of at most 0.0049.
Values may be sent and summed in bfloat16 or wider, within the bound.
A program may use at most 32 MiB of HBM per device.

v0:
```python
import jax
import jax.numpy as jnp
from jax import lax
from jax.sharding import PartitionSpec as P


def with_halo(block, sides, width):
    for axis, dim in sides:
        count = lax.axis_size(axis)
        forward = [(i, i + 1) for i in range(count - 1)]
        backward = [(target, source) for source, target in forward]
        low = lax.ppermute(
            lax.slice_in_dim(block, block.shape[dim] - width, None, axis=dim), axis, forward
        )
        high = lax.ppermute(lax.slice_in_dim(block, 0, width, axis=dim), axis, backward)
        block = jnp.concatenate([low, block, high], axis=dim)
    return block


def per_device(a_cols, a_blocks, p_blocks, send_rows):
    local_rows, per_row = a_cols.shape
    block_size = p_blocks.shape[1]
    block_span = p_blocks.shape[2]
    dom_size = lax.axis_size("dom")
    dom_place = lax.axis_index("dom")
    slot_count = send_rows.shape[1]
    flat_codes = a_cols.reshape(-1)
    near_count = 3 * local_rows
    nearby = with_halo(p_blocks, (("sub", 0),), local_rows)
    near_blocks = jnp.take(nearby, jnp.clip(flat_codes, 0, near_count - 1), axis=0)
    remote_index = jnp.clip(flat_codes - near_count, 0, dom_size * slot_count - 1)
    source_peer = remote_index // slot_count
    every_rows, every_lists = (
        lax.all_gather(p_blocks, "dom", axis=0, tiled=True),
        lax.all_gather(send_rows, "dom", axis=0, tiled=True),
    )
    peer_slot = remote_index % slot_count
    listed_row = every_lists[source_peer * dom_size + dom_place, peer_slot]
    far_index = source_peer * local_rows + jnp.clip(listed_row, 0, local_rows - 1)
    far_blocks = jnp.take(every_rows, far_index, axis=0)
    picked = jnp.where((flat_codes < near_count)[:, None, None], near_blocks, far_blocks)
    picked = picked.reshape(local_rows, per_row, block_size, block_span)
    window_group = jnp.where(
        flat_codes < local_rows,
        dom_size,
        jnp.where(
            flat_codes < 2 * local_rows,
            dom_place,
            jnp.where(flat_codes < near_count, dom_size + 1, source_peer),
        ),
    )
    sections = dom_size + 2
    member = (window_group[:, None] == jnp.arange(sections)[None, :]).astype(jnp.float32)
    member = member.reshape(local_rows, per_row, sections)

    def one_row(operands):
        coupled_a, coupled_p, row_member = operands
        products = jnp.einsum(
            "kab,kbc->kac", coupled_a, coupled_p, preferred_element_type=jnp.float32
        )
        summed = jnp.einsum("kt,kbc->tbc", row_member, products, precision=lax.Precision.HIGHEST)
        return (
            jnp.transpose(summed, (1, 0, 2))
            .reshape(block_size, sections * block_span)
            .astype(jnp.bfloat16)
        )

    fine_coarse = lax.map(one_row, (a_blocks, picked, member))
    coarse = lax.dot_general(
        p_blocks.reshape(local_rows * block_size, block_span),
        fine_coarse.reshape(local_rows * block_size, sections * block_span),
        (((0,), (0,)), ((), ())),
        preferred_element_type=jnp.float32,
    )
    return coarse.reshape(block_span // block_size, block_size, sections * block_span).astype(
        jnp.bfloat16
    )


def solution(mesh):
    placed = (
        P(("sub", "dom"), None),
        P(("sub", "dom"), None, None, None),
        P(("sub", "dom"), None, None),
        P(("sub", "dom"), None),
    )
    return jax.shard_map(
        per_device,
        mesh=mesh,
        in_specs=placed,
        out_specs=P(("sub", "dom"), None, None),
        check_vma=False,
    )
```

profile of v0, /device:TPU:1, one launch (start us, length us, event | category | flops | bytes accessed | tf_op | source)
XLA Modules:
  0.0 132.6 jit_solution(7574764492147055132)
XLA Ops:
  6.5 0.7 all-gather.2.cloned.1.call-update
  7.3 4.9 %collective-permute-start = (bf16[3,128,128]{2,1,0:T(8,128)(2,1)}, bf16[3,128,128]{2,1,0:T(8,128)(2,1)S(1)}, u32[]{:S(2)}, u32[]{:S(2)}) collective-permute-start(bf16[3,128,128]{2,1,0:T(8,128)(2,1)} %param.8), channel_id=1, source_target_pairs={{0,16},{16,32},{32,48},{48,64},{64,80},{80,96},{96,112},{112,128},... | collective-permute-start | bytes 294920 | tf_op jit(solution)/shard_map/ppermute | solution.py:12
  12.2 12.4 %collective-permute-start.1 = (bf16[3,128,128]{2,1,0:T(8,128)(2,1)}, bf16[3,128,128]{2,1,0:T(8,128)(2,1)S(1)}, u32[]{:S(2)}, u32[]{:S(2)}) collective-permute-start(bf16[3,128,128]{2,1,0:T(8,128)(2,1)} %param.8), channel_id=1, source_target_pairs={{16,0},{32,16},{48,32},{64,48},{80,64},{96,80},{112,96},{128,112},... | collective-permute-start | bytes 294920 | tf_op jit(solution)/shard_map/ppermute | solution.py:15
  24.7 0.7 broadcast_clamp_fusion
  25.3 0.1 add.127
  25.4 0.1 mul.33
  25.5 1.3 %dynamic-slice = u32[1]{0:T(128)} dynamic-slice(u32[1024]{0:T(1024)} %constant.120, u32[]{:T(128)S(6)} %add.136), dynamic_slice_sizes={1} | dynamic-slice | bytes 12
  27.5 0.8 bitcast_dynamic-update-slice_fusion
  28.2 5.6 %all-reduce.1 = s32[256]{0:T(256)S(1)} all-reduce(s32[256]{0:T(256)S(1)} %bitcast_dynamic-update-slice_fusion), channel_id=1, replica_groups=mesh['sub'=64,'dom'=16] {'dom'}, use_global_device_ids=true, to_apply=%add.1 | all-reduce | flops 256 | bytes 2048
  33.8 1.5 %gather_fusion.1 = s32[81]{0:T(128)S(1)} fusion(s32[256,1]{0,1:T(1,128)S(1)} %bitcast.51, s32[81]{0:T(128)S(1)} %fusion.24), kind=kCustom, calls=%fused_computation.1 | custom fusion | bytes 1296 | tf_op jit(solution)/shard_map/gather | solution.py:38
  35.3 0.1 min.33
  35.5 0.7 broadcast_compare_fusion
  36.3 0.9 pad_maximum_fusion
  37.2 1.1 gather_fusion
  38.3 60.5 %all-gather.2.cloned.1.call-done = bf16[48,128,128]{2,1,0:T(8,128)(2,1)} async-done(((bf16[3,128,128]{2,1,0:T(8,128)(2,1)}), bf16[48,128,128]{2,1,0:T(8,128)(2,1)}) %all-gather.2.cloned.1.call-update) | async-done | bytes 1572880 | tf_op jit(solution)/shard_map/all_gather | solution.py:34
  98.8 4.0 %gather_fusion.2 = bf16[81,128,128]{2,1,0:T(8,128)(2,1)} fusion(bf16[48,128,128]{2,1,0:T(8,128)(2,1)} %all-gather.2.cloned.1.call-done, s32[1024]{0:T(1024)S(1)} %pad_clamp_fusion), kind=kCustom, calls=%fused_computation.2 | custom fusion | bytes 5308740 | tf_op jit(solution)/shard_map/jit(_take)/gather | solution.py:40
  102.8 3.2 %select_select_fusion = bf16[3,27,128,128]{3,2,1,0:T(8,128)(2,1)} fusion(bf16[3,27,128,128]{3,2,1,0:T(8,128)(2,1)} %bitcast.54, bf16[3,27,128,128]{3,2,1,0:T(8,128)(2,1)S(1)} %bitcast.53, pred[3,27]{1,0:T(4,128)(4,1)S(1)} %get-tuple-element.44, pred[3,27]{1,0:T(4,128)(4,1)S(1)} %get-tuple-element.45, pred[3,27]{1,0:T(4,128)(4,1)S(1)} %get-tuple-element.43), kind=kLoop, calls=%fused_computation.20 | loop fusion | flops 3981312 | bytes 7962867 | tf_op jit(solution)/shard_map/jit(_where)/select_n | solution.py:41
  106.0 16.6 %while.10 = (s32[]{:T(128)}, bf16[3,128,2304]{1,2,0:T(8,128)(2,1)}, f32[3,27,18]{1,2,0:T(8,128)S(1)}, bf16[3,27,128,128]{3,2,1,0:T(8,128)(2,1)}, bf16[3,27,128,128]{3,2,1,0:T(8,128)(2,1)}, /*index=5*/s32[]{:T(128)}) while((s32[]{:T(128)}, bf16[3,128,2304]{1,2,0:T(8,128)(2,1)}, f32[3,27,18]{1,2,0:T(8,128)S(1)}, ...), condition=%wide.region_1.2_spmd, body=%wide.region_0.1_spmd.sunk | while | flops 209092608 | bytes 8271433 | solution.py:68
  106.0 1.8 %fusion.38 = f32[27,128,128]{2,1,0:T(8,128)S(1)} fusion(bf16[3,27,128,128]{3,2,1,0:T(8,128)(2,1)} %get-tuple-element.97, s32[]{:T(128)} %get-tuple-element.87, bf16[3,27,128,128]{3,2,1,0:T(8,128)(2,1)} %get-tuple-element.96), kind=kOutput, calls=%fused_computation.7.clone.1 | convolution fusion | flops 113246208 | bytes 3539968 | tf_op jit(solution)/shard_map/while/body/eval_jaxpr/kab,kbc->kac/dot_general | solution.py:58
  107.9 2.3 %fusion.39 = bf16[128,18,128]{2,1,0:T(8,128)(2,1)S(1)} fusion(f32[27,128,128]{2,1,0:T(8,128)S(1)} %fusion.38, f32[3,27,18]{1,2,0:T(8,128)S(1)} %get-tuple-element.95, s32[]{:T(128)} %get-tuple-element.87), kind=kOutput, calls=%fused_computation.6.clone.1 | convolution fusion | flops 95846400 | bytes 2371588 | tf_op jit(solution)/shard_map/while/body/eval_jaxpr/kt,kbc->tbc/dot_general | solution.py:61
  110.2 0.5 copy.25
  110.7 0.9 constant_dynamic-update-slice_fusion.2
  111.6 1.8 %fusion.38 = f32[27,128,128]{2,1,0:T(8,128)S(1)} fusion(bf16[3,27,128,128]{3,2,1,0:T(8,128)(2,1)} %get-tuple-element.97, s32[]{:T(128)} %get-tuple-element.87, bf16[3,27,128,128]{3,2,1,0:T(8,128)(2,1)} %get-tuple-element.96), kind=kOutput, calls=%fused_computation.7.clone.1 | convolution fusion | flops 113246208 | bytes 3539968 | tf_op jit(solution)/shard_map/while/body/eval_jaxpr/kab,kbc->kac/dot_general | solution.py:58
  113.4 2.3 %fusion.39 = bf16[128,18,128]{2,1,0:T(8,128)(2,1)S(1)} fusion(f32[27,128,128]{2,1,0:T(8,128)S(1)} %fusion.38, f32[3,27,18]{1,2,0:T(8,128)S(1)} %get-tuple-element.95, s32[]{:T(128)} %get-tuple-element.87), kind=kOutput, calls=%fused_computation.6.clone.1 | convolution fusion | flops 95846400 | bytes 2371588 | tf_op jit(solution)/shard_map/while/body/eval_jaxpr/kt,kbc->tbc/dot_general | solution.py:61
  115.8 0.5 copy.25
  116.2 0.9 constant_dynamic-update-slice_fusion.2
  117.1 1.8 %fusion.38 = f32[27,128,128]{2,1,0:T(8,128)S(1)} fusion(bf16[3,27,128,128]{3,2,1,0:T(8,128)(2,1)} %get-tuple-element.97, s32[]{:T(128)} %get-tuple-element.87, bf16[3,27,128,128]{3,2,1,0:T(8,128)(2,1)} %get-tuple-element.96), kind=kOutput, calls=%fused_computation.7.clone.1 | convolution fusion | flops 113246208 | bytes 3539968 | tf_op jit(solution)/shard_map/while/body/eval_jaxpr/kab,kbc->kac/dot_general | solution.py:58
  118.9 2.3 %fusion.39 = bf16[128,18,128]{2,1,0:T(8,128)(2,1)S(1)} fusion(f32[27,128,128]{2,1,0:T(8,128)S(1)} %fusion.38, f32[3,27,18]{1,2,0:T(8,128)S(1)} %get-tuple-element.95, s32[]{:T(128)} %get-tuple-element.87), kind=kOutput, calls=%fused_computation.6.clone.1 | convolution fusion | flops 95846400 | bytes 2371588 | tf_op jit(solution)/shard_map/while/body/eval_jaxpr/kt,kbc->tbc/dot_general | solution.py:61
  121.3 0.5 copy.25
  121.8 0.9 constant_dynamic-update-slice_fusion.2
  122.6 2.1 %fusion.18 = bf16[1,128,2304]{1,2,0:T(8,128)(2,1)S(1)} fusion(bf16[3,128,2304]{1,2,0:T(8,128)(2,1)} %get-tuple-element.32, bf16[3,128,128]{2,1,0:T(8,128)(2,1)S(1)} %copy-done), kind=kOutput, calls=%fused_computation.19 | convolution fusion | flops 226787328 | bytes 2457600 | tf_op jit(solution)/shard_map/dot_general | solution.py:69
  124.7 1.1 copy.15
  (15 shorter events, 0.1 us)
Async XLA Ops:
  6.5 92.3 %all-gather.2.cloned.1.call-start = ((), (), s32[]{:S(2)}) async-start(), calls=%async_computation | async-start | bytes 1671168 | tf_op jit(solution)/shard_map/all_gather | solution.py:34
  7.3 29.0 %collective-permute-start = (bf16[3,128,128]{2,1,0:T(8,128)(2,1)}, bf16[3,128,128]{2,1,0:T(8,128)(2,1)S(1)}, u32[]{:S(2)}, u32[]{:S(2)}) collective-permute-start(bf16[3,128,128]{2,1,0:T(8,128)(2,1)} %param.8), channel_id=1, source_target_pairs={{0,16},{16,32},{32,48},{48,64},{64,80},{80,96},{96,112},{112,128},... | collective-permute-start | bytes 294920 | tf_op jit(solution)/shard_map/ppermute | solution.py:12
  12.2 24.1 %collective-permute-start.1 = (bf16[3,128,128]{2,1,0:T(8,128)(2,1)}, bf16[3,128,128]{2,1,0:T(8,128)(2,1)S(1)}, u32[]{:S(2)}, u32[]{:S(2)}) collective-permute-start(bf16[3,128,128]{2,1,0:T(8,128)(2,1)} %param.8), channel_id=1, source_target_pairs={{16,0},{32,16},{48,32},{64,48},{80,64},{96,80},{112,96},{128,112},... | collective-permute-start | bytes 294920 | tf_op jit(solution)/shard_map/ppermute | solution.py:15
  106.0 16.6 %copy-start = (bf16[3,128,128]{2,1,0:T(8,128)(2,1)S(1)}, bf16[3,128,128]{2,1,0:T(8,128)(2,1)}, u32[]{:S(2)}) copy-start(bf16[3,128,128]{2,1,0:T(8,128)(2,1)} %param.8) | copy-start | bytes 294916
Sparse Core Ops, SparseCore 0:
  11.6 87.1 all-gather.1
where the time goes:
time: 133 us
  waiting for transfers between devices  61.3 us (46%)
  starting transfers between devices  17.4 us (13%)
  matrix products  14.6 us (11%)
  between operations  14.2 us (11%)
  local copies, waits for them, and re-layouts  14 us (11%)
  other arithmetic  5.6 us (4%)
  blocking collectives  5.56 us (4%)
    all_gather x1, waiting for transfers between devices, per_device(): lax.all_gather(p_blocks, 'dom', axis=0, tiled=True)  60.5 us
    ppermute x1, starting transfers between devices, with_halo(): lax.ppermute(lax.slice_in_dim(block, 0, width, axis=dim), axis, backward)  12.4 us
    dot_general x3, matrix products, one_row(): jnp.einsum('kt,kbc->tbc', row_member, products, precision=lax.Precision.H...  7.04 us
    unnamed x1, blocking collectives  5.56 us
    dot_general x3, matrix products, one_row(): jnp.einsum('kab,kbc->kac', coupled_a, coupled_p, preferred_element_type=j...  5.48 us
    ppermute x1, starting transfers between devices, with_halo(): lax.ppermute(lax.slice_in_dim(block, block.shape[dim] - width, None, axis...  4.94 us
    gather x1, local copies, waits for them, and re-layouts, per_device(): far_blocks = jnp.take(every_rows, far_index, axis=0)  3.96 us
    select_n x1, other arithmetic, per_device(): jnp.where((flat_codes < near_count)[:, None, None], near_blocks, far_blocks)  3.24 us
  transfers between devices with their start and end apart: 3, of which 1 were waited for; matrix products, arithmetic and copies ran while one was open for 6% of the time, Pallas kernels for 0%

commit v1 on v0

v1 whole, which is shorter than its diff:
```python
import functools

import jax
import jax.numpy as jnp
from jax import lax
from jax.experimental import pallas as pl
from jax.experimental.pallas import tpu as pltpu
from jax.sharding import PartitionSpec as P

MESH = pl.DeviceIdType.MESH
F32 = jnp.float32
BF16 = jnp.bfloat16


def kernel(
    n_sub, n_dom, rows, per_row, size,
    cols, send_rows, a_hbm, p_hbm, out,
    a_buf, p_buf, stage, far, near, part, pairs, table, links,
    a_sem, p_sem, link_sem, far_send, far_recv, near_send, near_recv,
):
    sub, dom = lax.axis_index("sub"), lax.axis_index("dom")
    above, below = lax.rem(sub + 1, n_sub), lax.rem(sub + n_sub - 1, n_sub)
    items = rows * per_row
    codes = 3 * rows + n_dom

    barrier = pltpu.get_barrier_semaphore()
    for step in range(1, n_dom):
        peer = lax.rem(dom + step, n_dom)
        pl.semaphore_signal(barrier, inc=1, device_id={"dom": peer}, device_id_type=MESH)
    for other in (above, below):
        pl.semaphore_signal(barrier, inc=1, device_id={"sub": other}, device_id_type=MESH)

    p_copy = pltpu.make_async_copy(p_hbm, p_buf, p_sem)
    p_copy.start()
    a_copies = [
        pltpu.make_async_copy(a_hbm.at[r], a_buf.at[r], a_sem.at[r]) for r in range(rows)
    ]
    for copy in a_copies:
        copy.start()

    lane = lax.broadcasted_iota(jnp.int32, (1, 128), 1)
    last = jnp.full((1, 128), items, jnp.int32)
    for j in range(items):
        table[pl.ds(j, 1), :] = last
        last = jnp.where(lane == cols[j // per_row, j % per_row], j, last)
    table[pl.ds(items, 1), :] = last
    link_copy = pltpu.make_async_copy(table, links, link_sem)
    link_copy.start()

    p_copy.wait()
    for step in range(1, n_dom):
        peer = lax.rem(dom + step, n_dom)
        row = jnp.clip(send_rows[peer], 0, rows - 1)
        stage[step] = p_buf[row]

    pl.semaphore_wait(barrier, n_dom + 1)
    far_copies = []
    for step in range(1, n_dom):
        peer = lax.rem(dom + step, n_dom)
        far_copies.append(
            pltpu.make_async_remote_copy(
                src_ref=stage.at[step], dst_ref=far.at[step],
                send_sem=far_send.at[step], recv_sem=far_recv.at[step],
                device_id={"dom": peer}, device_id_type=MESH,
            )
        )
        far_copies[-1].start()
    near_copies = []
    for place, other in ((0, above), (1, below)):
        near_copies.append(
            pltpu.make_async_remote_copy(
                src_ref=p_buf, dst_ref=near.at[place],
                send_sem=near_send.at[place], recv_sem=near_recv.at[place],
                device_id={"sub": other}, device_id_type=MESH,
            )
        )
        near_copies[-1].start()

    for r in range(rows):
        left = p_buf[r].T
        a_copies[r].wait()
        group = next(g for g in (9, 8, 6, 5, 4, 3, 2, 1) if per_row % g == 0)

        @pl.loop(0, per_row // group)
        def _(block):
            base = block * group
            for k in range(group):
                part[r * per_row + base + k] = jnp.dot(
                    left, a_buf[r, base + k], preferred_element_type=F32
                )

    part[items] = jnp.zeros((size, size), F32)
    link_copy.wait()
    for r in range(rows):

        @pl.loop(0, per_row)
        def _(k):
            j = r * per_row + k
            part[j] += part[links[j, cols[r, k]]]

    @pl.loop(0, codes)
    def _(v):
        total = part[links[items, v]]
        high = total.astype(BF16)
        low = (total - high.astype(F32)).astype(BF16)
        pairs[v] = jnp.concatenate([high, low], axis=1)

    def window(first, blocks):
        left = jnp.concatenate([pairs[first + i] for i in range(len(blocks))], axis=1)
        right = jnp.concatenate([b for b in blocks for _ in range(2)], axis=0)
        return jnp.dot(left, right, preferred_element_type=F32).astype(BF16)

    def put(place, value):
        out[0, :, pl.ds(pl.multiple_of(place * size, size), size)] = value

    put(dom, window(rows, [p_buf[r] for r in range(rows)]))
    for place in range(2):
        near_copies[place].wait()
        put(n_dom + place, window(2 * rows * place, [near[place, r] for r in range(rows)]))
    for step in range(1, n_dom):
        far_copies[step - 1].wait()
        source = lax.rem(dom + n_dom - step, n_dom)
        put(source, window(3 * rows + source, [far[step]]))


def per_device(n_sub, n_dom, a_cols, a_blocks, p_blocks, send_rows):
    rows, per_row = a_cols.shape
    size = p_blocks.shape[1]
    items = rows * per_row
    table_rows = (items + 8) // 8 * 8
    block = (size, size)
    dma = pltpu.SemaphoreType.DMA
    return pl.pallas_call(
        functools.partial(kernel, n_sub, n_dom, rows, per_row, size),
        out_shape=jax.ShapeDtypeStruct((1, size, (n_dom + 2) * size), BF16),
        in_specs=[
            pl.BlockSpec(memory_space=pltpu.SMEM),
            pl.BlockSpec(memory_space=pltpu.SMEM),
            pl.BlockSpec(memory_space=pltpu.HBM),
            pl.BlockSpec(memory_space=pltpu.HBM),
        ],
        out_specs=pl.BlockSpec(memory_space=pltpu.VMEM),
        scratch_shapes=[
            pltpu.VMEM((rows, per_row) + block, BF16),
            pltpu.VMEM((rows,) + block, BF16),
            pltpu.VMEM((n_dom,) + block, BF16),
            pltpu.VMEM((n_dom,) + block, BF16),
            pltpu.VMEM((2, rows) + block, BF16),
            pltpu.VMEM((items + 1,) + block, F32),
            pltpu.VMEM((3 * rows + n_dom, size, 2 * size), BF16),
            pltpu.VMEM((table_rows, 128), jnp.int32),
            pltpu.SMEM((table_rows, 128), jnp.int32),
            dma((rows,)), dma, dma,
            dma((n_dom,)), dma((n_dom,)), dma((2,)), dma((2,)),
        ],
        compiler_params=pltpu.CompilerParams(
            collective_id=0, has_side_effects=True, vmem_limit_bytes=60 * 1024 * 1024
        ),
        cost_estimate=pl.CostEstimate(
            flops=2 * (items + 2 * codes_of(rows, n_dom)) * size**3,
            bytes_accessed=2 * size * size * (items + rows + n_dom + 2),
            transcendentals=0,
        ),
    )(a_cols, send_rows.reshape(-1), a_blocks, p_blocks)


def codes_of(rows, n_dom):
    return 3 * rows + n_dom


def solution(mesh):
    placed = (
        P(("sub", "dom"), None),
        P(("sub", "dom"), None, None, None),
        P(("sub", "dom"), None, None),
        P(("sub", "dom"), None),
    )
    return jax.shard_map(
        functools.partial(per_device, mesh.shape["sub"], mesh.shape["dom"]),
        mesh=mesh,
        in_specs=placed,
        out_specs=P(("sub", "dom"), None, None),
        check_vma=False,
    )
```

time: 133 us -> 31.2 us (0.23)
  the two profiles are of different devices: /device:TPU:1 before, /device:TPU:8 now
where the time goes in v1:
time: 31.2 us; the launch traced here: 31 us
  Pallas kernels  29.1 us (93%)
  local copies, waits for them, and re-layouts  1.92 us (6%)
    pallas_call x1, Pallas kernels, per_device(): pl.pallas_call(functools.partial(kernel, n_sub, n_dom, rows, per_row, siz...  29.1 us
    unnamed x1, local copies, waits for them, and re-layouts  1.92 us

profile of v1, /device:TPU:8, one launch (start us, length us, event | category | flops | bytes accessed | tf_op | source)
XLA Modules:
  0.0 31.0 jit_solution(15791021512121006068)
XLA Ops:
  0.0 29.1 %shard_map.46 = bf16[1,128,2304]{2,1,0:T(8,128)(2,1)} custom-call(s32[3,27]{1,0:T(4,128)} %cols.1, s32[16]{0:T(128)} %bitcast.1, bf16[3,27,128,128]{3,2,1,0:T(8,128)(2,1)} %a_hbm.1, bf16[3,128,128]{2,1,0:T(8,128)(2,1)} %p_hbm.1), custom_call_target="tpu_custom_call" | custom-call | flops 549453824 | bytes 3342336 | tf_op jit(solution)/shard_map/pallas_call | solution.py:133
  29.1 1.9 %copy.6 = bf16[1,128,2304]{2,1,0:T(8,128)(2,1)} copy(bf16[1,128,2304]{2,1,0:T(8,128)(2,1)} %shard_map.46) | data formatting | bytes 1179648

commit v2 on v1

--- a/solution.py
+++ b/solution.py
@@ -16,19 +16,26 @@
     n_sub, n_dom, rows, per_row, size,
     cols, send_rows, a_hbm, p_hbm, out,
     a_buf, p_buf, stage, far, near, part, pairs, table, links,
-    a_sem, p_sem, link_sem, far_send, far_recv, near_send, near_recv,
+    a_sem, p_sem, link_sem, far_send, far_recv, near_send, near_recv, root_in,
 ):
     sub, dom = lax.axis_index("sub"), lax.axis_index("dom")
-    above, below = lax.rem(sub + 1, n_sub), lax.rem(sub + n_sub - 1, n_sub)
     items = rows * per_row
     codes = 3 * rows + n_dom
 
+    root = (sub == 0) & (dom == 0)
+    has_below, has_above = sub > 0, sub < n_sub - 1
+    root_far = (sub == 0) & (dom > 0)
+    root_near = (sub == 1) & (dom == 0)
+    meets_root = root_far | root_near
+    one = jnp.int32(1)
+
+    def count(flag):
+        return jnp.where(flag, one, 0)
+
     barrier = pltpu.get_barrier_semaphore()
-    for step in range(1, n_dom):
-        peer = lax.rem(dom + step, n_dom)
-        pl.semaphore_signal(barrier, inc=1, device_id={"dom": peer}, device_id_type=MESH)
-    for other in (above, below):
-        pl.semaphore_signal(barrier, inc=1, device_id={"sub": other}, device_id_type=MESH)
+
+    def greet(other):
+        pl.semaphore_signal(barrier, inc=1, device_id=other, device_id_type=MESH)
 
     p_copy = pltpu.make_async_copy(p_hbm, p_buf, p_sem)
     p_copy.start()
@@ -37,6 +44,85 @@
     ]
     for copy in a_copies:
         copy.start()
+
+    @pl.when(jnp.logical_not(root))
+    def _():
+        for step in range(1, n_dom):
+            peer = lax.rem(dom + step, n_dom)
+
+            @pl.when(jnp.logical_not((sub == 0) & (peer == 0)))
+            def _():
+                greet({"dom": peer})
+
+        @pl.when(has_above)
+        def _():
+            greet({"sub": sub + 1})
+
+        @pl.when(has_below & jnp.logical_not(root_near))
+        def _():
+            greet({"sub": sub - 1})
+
+    p_copy.wait()
+
+    @pl.loop(1, n_dom)
+    def _(step):
+        row = jnp.clip(send_rows[lax.rem(dom + step, n_dom)], 0, rows - 1)
+        stage[step] = p_buf[row]
+
+    def far_copy(step):
+        return pltpu.make_async_remote_copy(
+            src_ref=stage.at[step], dst_ref=far.at[step],
+            send_sem=far_send.at[step], recv_sem=far_recv.at[step],
+            device_id={"dom": lax.rem(dom + step, n_dom)}, device_id_type=MESH,
+        )
+
+    def near_copy(place):
+        return pltpu.make_async_remote_copy(
+            src_ref=p_buf, dst_ref=near.at[place],
+            send_sem=near_send.at[place], recv_sem=near_recv.at[place],
+            device_id={"sub": sub + 1 - 2 * place}, device_id_type=MESH,
+        )
+
+    def to_root(step):
+        return (sub == 0) & (lax.rem(dom + step, n_dom) == 0)
+
+    def from_root(step):
+        return (sub == 0) & (dom == step)
+
+    @pl.when(root)
+    def _():
+        pl.semaphore_wait(barrier, n_dom)
+        for step in range(1, n_dom):
+            pl.semaphore_signal(root_in, inc=1, device_id={"dom": dom + step}, device_id_type=MESH)
+        pl.semaphore_signal(root_in, inc=1, device_id={"sub": sub + 1}, device_id_type=MESH)
+
+    @pl.when(jnp.logical_not(root))
+    def _():
+        pl.semaphore_wait(
+            barrier, n_dom - 1 + count(has_above) + count(has_below) - count(meets_root)
+        )
+
+    @pl.when(root_far)
+    def _():
+        greet({"dom": 0})
+
+    @pl.when(root_near)
+    def _():
+        greet({"sub": 0})
+
+    @pl.loop(1, n_dom)
+    def _(step):
+        @pl.when(jnp.logical_not(to_root(step)))
+        def _():
+            far_copy(step).start()
+
+    @pl.when(has_above)
+    def _():
+        near_copy(0).start()
+
+    @pl.when(has_below & jnp.logical_not(root_near))
+    def _():
+        near_copy(1).start()
 
     lane = lax.broadcasted_iota(jnp.int32, (1, 128), 1)
     last = jnp.full((1, 128), items, jnp.int32)
@@ -47,35 +133,6 @@
     link_copy = pltpu.make_async_copy(table, links, link_sem)
     link_copy.start()
 
-    p_copy.wait()
-    for step in range(1, n_dom):
-        peer = lax.rem(dom + step, n_dom)
-        row = jnp.clip(send_rows[peer], 0, rows - 1)
-        stage[step] = p_buf[row]
-
-    pl.semaphore_wait(barrier, n_dom + 1)
-    far_copies = []
-    for step in range(1, n_dom):
-        peer = lax.rem(dom + step, n_dom)
-        far_copies.append(
-            pltpu.make_async_remote_copy(
-                src_ref=stage.at[step], dst_ref=far.at[step],
-                send_sem=far_send.at[step], recv_sem=far_recv.at[step],
-                device_id={"dom": peer}, device_id_type=MESH,
-            )
-        )
-        far_copies[-1].start()
-    near_copies = []
-    for place, other in ((0, above), (1, below)):
-        near_copies.append(
-            pltpu.make_async_remote_copy(
-                src_ref=p_buf, dst_ref=near.at[place],
-                send_sem=near_send.at[place], recv_sem=near_recv.at[place],
-                device_id={"sub": other}, device_id_type=MESH,
-            )
-        )
-        near_copies[-1].start()
-
     for r in range(rows):
         left = p_buf[r].T
         a_copies[r].wait()
@@ -114,13 +171,63 @@
         out[0, :, pl.ds(pl.multiple_of(place * size, size), size)] = value
 
     put(dom, window(rows, [p_buf[r] for r in range(rows)]))
-    for place in range(2):
-        near_copies[place].wait()
+
+    def take_near(place):
+        near_copy(place).wait_recv()
         put(n_dom + place, window(2 * rows * place, [near[place, r] for r in range(rows)]))
-    for step in range(1, n_dom):
-        far_copies[step - 1].wait()
+
+    def take_far(step):
+        far_copy(step).wait_recv()
         source = lax.rem(dom + n_dom - step, n_dom)
         put(source, window(3 * rows + source, [far[step]]))
+
+    @pl.when(has_below & jnp.logical_not(root_near))
+    def _():
+        take_near(0)
+
+    @pl.when(has_above)
+    def _():
+        take_near(1)
+
+    for place, there in ((0, has_below), (1, has_above)):
+
+        @pl.when(jnp.logical_not(there))
+        def _():
+            put(n_dom + place, jnp.zeros((size, size), BF16))
+
+    @pl.loop(1, n_dom)
+    def _(step):
+        @pl.when(jnp.logical_not(from_root(step)))
+        def _():
+            take_far(step)
+
+    @pl.loop(1, n_dom)
+    def _(step):
+        @pl.when(jnp.logical_not(to_root(step)))
+        def _():
+            far_copy(step).wait_send()
+
+    @pl.when(has_above)
+    def _():
+        near_copy(0).wait_send()
+
+    @pl.when(has_below & jnp.logical_not(root_near))
+    def _():
+        near_copy(1).wait_send()
+
+    @pl.when(root_far)
+    def _():
+        pl.semaphore_wait(root_in, 1)
+        far_copy(n_dom - dom).start()
+        take_far(dom)
+        far_copy(n_dom - dom).wait_send()
+
+    @pl.when(root_near)
+    def _():
+        pl.semaphore_wait(root_in, 1)
+        near_copy(1).start()
+        take_near(0)
+        near_copy(1).wait_send()
 
 
 def per_device(n_sub, n_dom, a_cols, a_blocks, p_blocks, send_rows):
@@ -130,6 +237,7 @@
     table_rows = (items + 8) // 8 * 8
     block = (size, size)
     dma = pltpu.SemaphoreType.DMA
+    operands = (a_cols, send_rows.reshape(-1), a_blocks, p_blocks)
     return pl.pallas_call(
         functools.partial(kernel, n_sub, n_dom, rows, per_row, size),
         out_shape=jax.ShapeDtypeStruct((1, size, (n_dom + 2) * size), BF16),
@@ -151,17 +259,17 @@
             pltpu.VMEM((table_rows, 128), jnp.int32),
             pltpu.SMEM((table_rows, 128), jnp.int32),
             dma((rows,)), dma, dma,
-            dma((n_dom,)), dma((n_dom,)), dma((2,)), dma((2,)),
+            dma((n_dom,)), dma((n_dom,)), dma((2,)), dma((2,)), pltpu.SemaphoreType.REGULAR,
         ],
         compiler_params=pltpu.CompilerParams(
-            collective_id=0, has_side_effects=True, vmem_limit_bytes=60 * 1024 * 1024
+            collective_id=0, has_side_effects=True, vmem_limit_bytes=48 * 1024 * 1024
         ),
         cost_estimate=pl.CostEstimate(
             flops=2 * (items + 2 * codes_of(rows, n_dom)) * size**3,
             bytes_accessed=2 * size * size * (items + rows + n_dom + 2),
             transcendentals=0,
         ),
-    )(a_cols, send_rows.reshape(-1), a_blocks, p_blocks)
+    )(*(pltpu.with_memory_space_constraint(x, pltpu.HBM) for x in operands))
 
 
 def codes_of(rows, n_dom):

time: 31.2 us -> 21.9 us (0.70)
  the two profiles are of different devices: /device:TPU:8 before, /device:TPU:28 now
where the time goes in v2:
time: 21.9 us; the launch traced here: 21.7 us
  Pallas kernels  20.9 us (95%)
  local copies, waits for them, and re-layouts  0.82 us (4%)
    pallas_call x1, Pallas kernels, per_device(): pl.pallas_call(functools.partial(kernel, n_sub, n_dom, rows, per_row, siz...  20.9 us
    unnamed x1, local copies, waits for them, and re-layouts  0.82 us

profile of v2, /device:TPU:28, one launch (start us, length us, event | category | flops | bytes accessed | tf_op | source)
XLA Modules:
  0.0 21.7 jit_solution(1629610976642965620)
XLA Ops:
  0.0 20.9 %shard_map.46 = bf16[1,128,2304]{2,1,0:T(8,128)(2,1)S(1)} custom-call(s32[3,27]{1,0:T(4,128)} %cols.1, s32[16]{0:T(128)} %bitcast.1, bf16[3,27,128,128]{3,2,1,0:T(8,128)(2,1)} %a_hbm.1, bf16[3,128,128]{2,1,0:T(8,128)(2,1)} %p_hbm.1), custom_call_target="tpu_custom_call" | custom-call | flops 549453824 | bytes 3342336 | tf_op jit(solution)/shard_map/pallas_call | solution.py:241
  20.9 0.8 %copy.6 = bf16[1,128,2304]{2,1,0:T(8,128)(2,1)} copy(bf16[1,128,2304]{2,1,0:T(8,128)(2,1)S(1)} %shard_map.46) | data formatting | bytes 1179648

commit v3 on v2

--- a/solution.py
+++ b/solution.py
@@ -12,15 +12,37 @@
 BF16 = jnp.bfloat16
 
 
+def far_first(size):
+    return sorted(range(size), key=lambda k: (-min(k, size - k), k))
+
+
+def near_first(long_side, side):
+    def order(offset):
+        x, y = offset // side, offset % side
+        steps = min(x, long_side - x) + min(y, side - y)
+        return (2 if x == 0 else int(x > long_side // 2), steps, offset)
+
+    return sorted(range(1, long_side * side), key=order)
+
+
+def pick(values, i):
+    value = jnp.int32(values[-1])
+    for k, v in enumerate(values[:-1]):
+        value = jnp.where(i == k, jnp.int32(v), value)
+    return value
+
+
 def kernel(
     n_sub, n_dom, rows, per_row, size,
-    cols, send_rows, a_hbm, p_hbm, out,
-    a_buf, p_buf, stage, far, near, part, pairs, table, links,
-    a_sem, p_sem, link_sem, far_send, far_recv, near_send, near_recv, root_in,
+    cols_hbm, send_hbm, a_hbm, p_hbm, out,
+    cols, send_rows, a_buf, p_buf, stage, far, near, part, pairs, table, links,
+    cols_sem, send_rows_sem, a_sem, p_sem, link_sem, far_send, far_recv, near_send, near_recv, root_in,
 ):
     sub, dom = lax.axis_index("sub"), lax.axis_index("dom")
     items = rows * per_row
     codes = 3 * rows + n_dom
+    side = max(k for k in range(1, n_dom + 1) if n_dom % k == 0 and k * k <= n_dom)
+    long_side = n_dom // side
 
     root = (sub == 0) & (dom == 0)
     has_below, has_above = sub > 0, sub < n_sub - 1
@@ -37,13 +59,24 @@
     def greet(other):
         pl.semaphore_signal(barrier, inc=1, device_id=other, device_id_type=MESH)
 
-    p_copy = pltpu.make_async_copy(p_hbm, p_buf, p_sem)
-    p_copy.start()
+    send_rows_copy = pltpu.make_async_copy(send_hbm, send_rows, send_rows_sem)
+    send_rows_copy.start()
+    half = size // 2
+    p_copies = [
+        pltpu.make_async_copy(
+            p_hbm.at[r, pl.ds(h * half, half)], p_buf.at[r, pl.ds(h * half, half)],
+            p_sem.at[2 * r + h],
+        )
+        for r in range(rows)
+        for h in range(2)
+    ]
+    for copy in p_copies:
+        copy.start()
+    cols_copy = pltpu.make_async_copy(cols_hbm, cols, cols_sem)
+    cols_copy.start()
     a_copies = [
         pltpu.make_async_copy(a_hbm.at[r], a_buf.at[r], a_sem.at[r]) for r in range(rows)
     ]
-    for copy in a_copies:
-        copy.start()
 
     @pl.when(jnp.logical_not(root))
     def _():
@@ -62,18 +95,23 @@
         def _():
             greet({"sub": sub - 1})
 
-    p_copy.wait()
-
-    @pl.loop(1, n_dom)
-    def _(step):
-        row = jnp.clip(send_rows[lax.rem(dom + step, n_dom)], 0, rows - 1)
-        stage[step] = p_buf[row]
-
-    def far_copy(step):
+    def peer_at(offset, sign):
+        x = lax.rem(dom // side + long_side + sign * (offset // side), long_side)
+        y = lax.rem(dom % side + side + sign * (offset % side), side)
+        return x * side + y
+
+    def offset_at(i):
+        return pick(far_first(long_side), i // side) * side + pick(far_first(side), i % side)
+
+    def put_on_stage(offset):
+        row = jnp.clip(send_rows[peer_at(offset, 1)], 0, rows - 1)
+        stage[offset] = p_buf[row]
+
+    def far_copy(offset):
         return pltpu.make_async_remote_copy(
-            src_ref=stage.at[step], dst_ref=far.at[step],
-            send_sem=far_send.at[step], recv_sem=far_recv.at[step],
-            device_id={"dom": lax.rem(dom + step, n_dom)}, device_id_type=MESH,
+            src_ref=stage.at[offset], dst_ref=far.at[offset],
+            send_sem=far_send.at[offset], recv_sem=far_recv.at[offset],
+            device_id={"dom": peer_at(offset, 1)}, device_id_type=MESH,
         )
 
     def near_copy(place):
@@ -83,47 +121,69 @@
             device_id={"sub": sub + 1 - 2 * place}, device_id_type=MESH,
         )
 
-    def to_root(step):
-        return (sub == 0) & (lax.rem(dom + step, n_dom) == 0)
-
-    def from_root(step):
-        return (sub == 0) & (dom == step)
+    def to_root(offset):
+        return (sub == 0) & (peer_at(offset, 1) == 0)
+
+    def from_root(offset):
+        return (sub == 0) & (dom == offset)
 
     @pl.when(root)
     def _():
         pl.semaphore_wait(barrier, n_dom)
         for step in range(1, n_dom):
-            pl.semaphore_signal(root_in, inc=1, device_id={"dom": dom + step}, device_id_type=MESH)
-        pl.semaphore_signal(root_in, inc=1, device_id={"sub": sub + 1}, device_id_type=MESH)
+            pl.semaphore_signal(root_in, inc=1, device_id={"dom": step}, device_id_type=MESH)
+        pl.semaphore_signal(root_in, inc=1, device_id={"sub": 1}, device_id_type=MESH)
+        send_rows_copy.wait()
+        for copy in p_copies:
+            copy.wait()
+        for offset in near_first(long_side, side):
+            put_on_stage(offset)
+            far_copy(offset).start()
+        near_copy(0).start()
+        for copy in a_copies:
+            copy.start()
 
     @pl.when(jnp.logical_not(root))
     def _():
+        for copy in a_copies:
+            copy.start()
+        send_rows_copy.wait()
+        for copy in p_copies:
+            copy.wait()
+
+        @pl.loop(1, n_dom)
+        def _(offset):
+            put_on_stage(offset)
+
         pl.semaphore_wait(
             barrier, n_dom - 1 + count(has_above) + count(has_below) - count(meets_root)
         )
 
-    @pl.when(root_far)
-    def _():
-        greet({"dom": 0})
-
-    @pl.when(root_near)
-    def _():
-        greet({"sub": 0})
-
-    @pl.loop(1, n_dom)
-    def _(step):
-        @pl.when(jnp.logical_not(to_root(step)))
-        def _():
-            far_copy(step).start()
-
-    @pl.when(has_above)
-    def _():
-        near_copy(0).start()
-
-    @pl.when(has_below & jnp.logical_not(root_near))
-    def _():
-        near_copy(1).start()
-
+        @pl.when(root_far)
+        def _():
+            greet({"dom": 0})
+
+        @pl.when(root_near)
+        def _():
+            greet({"sub": 0})
+
+        @pl.loop(0, n_dom - 1)
+        def _(i):
+            offset = offset_at(i)
+
+            @pl.when(jnp.logical_not(to_root(offset)))
+            def _():
+                far_copy(offset).start()
+
+        @pl.when(has_above)
+        def _():
+            near_copy(0).start()
+
+        @pl.when(has_below & jnp.logical_not(root_near))
+        def _():
+            near_copy(1).start()
+
+    cols_copy.wait()
     lane = lax.broadcasted_iota(jnp.int32, (1, 128), 1)
     last = jnp.full((1, 128), items, jnp.int32)
     for j in range(items):
@@ -176,10 +236,10 @@
         near_copy(place).wait_recv()
         put(n_dom + place, window(2 * rows * place, [near[place, r] for r in range(rows)]))
 
-    def take_far(step):
-        far_copy(step).wait_recv()
-        source = lax.rem(dom + n_dom - step, n_dom)
-        put(source, window(3 * rows + source, [far[step]]))
+    def take_far(offset):
+        far_copy(offset).wait_recv()
+        source = peer_at(offset, -1)
+        put(source, window(3 * rows + source, [far[offset]]))
 
     @pl.when(has_below & jnp.logical_not(root_near))
     def _():
@@ -195,17 +255,19 @@
         def _():
             put(n_dom + place, jnp.zeros((size, size), BF16))
 
+    @pl.loop(0, n_dom - 1)
+    def _(i):
+        offset = offset_at(i)
+
+        @pl.when(jnp.logical_not(from_root(offset)))
+        def _():
+            take_far(offset)
+
     @pl.loop(1, n_dom)
-    def _(step):
-        @pl.when(jnp.logical_not(from_root(step)))
-        def _():
-            take_far(step)
-
-    @pl.loop(1, n_dom)
-    def _(step):
-        @pl.when(jnp.logical_not(to_root(step)))
-        def _():
-            far_copy(step).wait_send()
+    def _(offset):
+        @pl.when(jnp.logical_not(to_root(offset)))
+        def _():
+            far_copy(offset).wait_send()
 
     @pl.when(has_above)
     def _():
@@ -218,9 +280,12 @@
     @pl.when(root_far)
     def _():
         pl.semaphore_wait(root_in, 1)
-        far_copy(n_dom - dom).start()
+        back = (
+            lax.rem(long_side - dom // side, long_side) * side + lax.rem(side - dom % side, side)
+        )
+        far_copy(back).start()
         take_far(dom)
-        far_copy(n_dom - dom).wait_send()
+        far_copy(back).wait_send()
 
     @pl.when(root_near)
     def _():
@@ -241,14 +306,11 @@
     return pl.pallas_call(
         functools.partial(kernel, n_sub, n_dom, rows, per_row, size),
         out_shape=jax.ShapeDtypeStruct((1, size, (n_dom + 2) * size), BF16),
-        in_specs=[
-            pl.BlockSpec(memory_space=pltpu.SMEM),
-            pl.BlockSpec(memory_space=pltpu.SMEM),
-            pl.BlockSpec(memory_space=pltpu.HBM),
-            pl.BlockSpec(memory_space=pltpu.HBM),
-        ],
+        in_specs=[pl.BlockSpec(memory_space=pltpu.HBM)] * 4,
         out_specs=pl.BlockSpec(memory_space=pltpu.VMEM),
         scratch_shapes=[
+            pltpu.SMEM(operands[0].shape, jnp.int32),
+            pltpu.SMEM(operands[1].shape, jnp.int32),
             pltpu.VMEM((rows, per_row) + block, BF16),
             pltpu.VMEM((rows,) + block, BF16),
             pltpu.VMEM((n_dom,) + block, BF16),
@@ -258,7 +320,7 @@
             pltpu.VMEM((3 * rows + n_dom, size, 2 * size), BF16),
             pltpu.VMEM((table_rows, 128), jnp.int32),
             pltpu.SMEM((table_rows, 128), jnp.int32),
-            dma((rows,)), dma, dma,
+            dma, dma, dma((rows,)), dma((2 * rows,)), dma,
             dma((n_dom,)), dma((n_dom,)), dma((2,)), dma((2,)), pltpu.SemaphoreType.REGULAR,
         ],
         compiler_params=pltpu.CompilerParams(

time: 21.9 us -> 20.5 us (0.936)
  the two profiles are of different devices: /device:TPU:28 before, /device:TPU:20 now
where the time goes in v3:
time: 20.5 us; the launch traced here: 20.2 us
  Pallas kernels  19.4 us (95%)
  local copies, waits for them, and re-layouts  0.82 us (4%)
    pallas_call x1, Pallas kernels, per_device(): pl.pallas_call(functools.partial(kernel, n_sub, n_dom, rows, per_row, siz...  19.4 us
    unnamed x1, local copies, waits for them, and re-layouts  0.82 us

profile of v3, /device:TPU:20, one launch (start us, length us, event | category | flops | bytes accessed | tf_op | source)
XLA Modules:
  0.0 20.2 jit_solution(10525107007185462781)
XLA Ops:
  0.0 19.4 %shard_map.46 = bf16[1,128,2304]{2,1,0:T(8,128)(2,1)S(1)} custom-call(s32[3,27]{1,0:T(4,128)} %cols_hbm.1, s32[16]{0:T(128)} %bitcast.1, bf16[3,27,128,128]{3,2,1,0:T(8,128)(2,1)} %a_hbm.1, bf16[3,128,128]{2,1,0:T(8,128)(2,1)} %p_hbm.1), custom_call_target="tpu_custom_call" | custom-call | flops 549453824 | bytes 3342336 | tf_op jit(solution)/shard_map/pallas_call | solution.py:306
  19.4 0.8 %copy.6 = bf16[1,128,2304]{2,1,0:T(8,128)(2,1)} copy(bf16[1,128,2304]{2,1,0:T(8,128)(2,1)S(1)} %shard_map.46) | data formatting | bytes 1179648

commit v4 on v3

--- a/solution.py
+++ b/solution.py
@@ -107,10 +107,10 @@
         row = jnp.clip(send_rows[peer_at(offset, 1)], 0, rows - 1)
         stage[offset] = p_buf[row]
 
-    def far_copy(offset):
+    def far_copy(offset, sender=0):
         return pltpu.make_async_remote_copy(
             src_ref=stage.at[offset], dst_ref=far.at[offset],
-            send_sem=far_send.at[offset], recv_sem=far_recv.at[offset],
+            send_sem=far_send.at[sender], recv_sem=far_recv.at[offset],
             device_id={"dom": peer_at(offset, 1)}, device_id_type=MESH,
         )
 
@@ -255,37 +255,48 @@
         def _():
             put(n_dom + place, jnp.zeros((size, size), BF16))
 
-    @pl.loop(0, n_dom - 1)
+    def wait_far_sends(number):
+        pltpu.make_async_remote_copy(
+            src_ref=stage.at[pl.ds(1, number)], dst_ref=far.at[pl.ds(1, number)],
+            send_sem=far_send.at[0], recv_sem=far_recv.at[0],
+            device_id={"dom": peer_at(1, 1)}, device_id_type=MESH,
+        ).wait_send()
+
+    @pl.when(root_far)
+    def _():
+        wait_far_sends(n_dom - 2)
+
+    @pl.when(jnp.logical_not(root_far))
+    def _():
+        wait_far_sends(n_dom - 1)
+
+    @pl.when(has_above)
+    def _():
+        near_copy(0).wait_send()
+
+    @pl.when(has_below & jnp.logical_not(root_near))
+    def _():
+        near_copy(1).wait_send()
+
+    back = lax.rem(long_side - dom // side, long_side) * side + lax.rem(side - dom % side, side)
+
+    @pl.loop(0, n_dom)
     def _(i):
-        offset = offset_at(i)
-
-        @pl.when(jnp.logical_not(from_root(offset)))
+        last_turn = i == n_dom - 1
+        offset = jnp.where(last_turn, dom, offset_at(i))
+
+        @pl.when(last_turn & root_far)
+        def _():
+            pl.semaphore_wait(root_in, 1)
+            far_copy(back, 1).start()
+
+        @pl.when(jnp.where(last_turn, root_far, jnp.logical_not(from_root(offset))))
         def _():
             take_far(offset)
 
-    @pl.loop(1, n_dom)
-    def _(offset):
-        @pl.when(jnp.logical_not(to_root(offset)))
-        def _():
-            far_copy(offset).wait_send()
-
-    @pl.when(has_above)
-    def _():
-        near_copy(0).wait_send()
-
-    @pl.when(has_below & jnp.logical_not(root_near))
-    def _():
-        near_copy(1).wait_send()
-
     @pl.when(root_far)
     def _():
-        pl.semaphore_wait(root_in, 1)
-        back = (
-            lax.rem(long_side - dom // side, long_side) * side + lax.rem(side - dom % side, side)
-        )
-        far_copy(back).start()
-        take_far(dom)
-        far_copy(back).wait_send()
+        far_copy(back, 1).wait_send()
 
     @pl.when(root_near)
     def _():
@@ -321,7 +332,7 @@
             pltpu.VMEM((table_rows, 128), jnp.int32),
             pltpu.SMEM((table_rows, 128), jnp.int32),
             dma, dma, dma((rows,)), dma((2 * rows,)), dma,
-            dma((n_dom,)), dma((n_dom,)), dma((2,)), dma((2,)), pltpu.SemaphoreType.REGULAR,
+            dma((2,)), dma((n_dom,)), dma((2,)), dma((2,)), pltpu.SemaphoreType.REGULAR,
         ],
         compiler_params=pltpu.CompilerParams(
             collective_id=0, has_side_effects=True, vmem_limit_bytes=48 * 1024 * 1024

time: 20.5 us -> 20.3 us (level)
  no operation moved by 1% of the time
where the time goes in v4:
time: 20.3 us; the launch traced here: 20.1 us
  Pallas kernels  19.3 us (95%)
  local copies, waits for them, and re-layouts  0.82 us (4%)
    pallas_call x1, Pallas kernels, per_device(): pl.pallas_call(functools.partial(kernel, n_sub, n_dom, rows, per_row, siz...  19.3 us
    unnamed x1, local copies, waits for them, and re-layouts  0.82 us

profile of v4, /device:TPU:20, one launch (start us, length us, event | category | flops | bytes accessed | tf_op | source)
XLA Modules:
  0.0 20.1 jit_solution(11395812401492610968)
XLA Ops:
  0.0 19.3 %shard_map.46 = bf16[1,128,2304]{2,1,0:T(8,128)(2,1)S(1)} custom-call(s32[3,27]{1,0:T(4,128)} %cols_hbm.1, s32[16]{0:T(128)} %bitcast.1, bf16[3,27,128,128]{3,2,1,0:T(8,128)(2,1)} %a_hbm.1, bf16[3,128,128]{2,1,0:T(8,128)(2,1)} %p_hbm.1), custom_call_target="tpu_custom_call" | custom-call | flops 549453824 | bytes 3342336 | tf_op jit(solution)/shard_map/pallas_call | solution.py:317
  19.3 0.8 %copy.6 = bf16[1,128,2304]{2,1,0:T(8,128)(2,1)} copy(bf16[1,128,2304]{2,1,0:T(8,128)(2,1)S(1)} %shard_map.46) | data formatting | bytes 1179648

commit v5 on v4

--- a/solution.py
+++ b/solution.py
@@ -16,13 +16,16 @@
     return sorted(range(size), key=lambda k: (-min(k, size - k), k))
 
 
-def near_first(long_side, side):
+def root_order(long_side, side):
     def order(offset):
         x, y = offset // side, offset % side
-        steps = min(x, long_side - x) + min(y, side - y)
-        return (2 if x == 0 else int(x > long_side // 2), steps, offset)
+        return (2 if x == 0 else int(x > long_side // 2), y, x)
 
     return sorted(range(1, long_side * side), key=order)
+
+
+def long_side_of(n_dom):
+    return min(k for k in range(1, n_dom + 1) if n_dom % k == 0 and k * k >= n_dom)
 
 
 def pick(values, i):
@@ -41,8 +44,8 @@
     sub, dom = lax.axis_index("sub"), lax.axis_index("dom")
     items = rows * per_row
     codes = 3 * rows + n_dom
-    side = max(k for k in range(1, n_dom + 1) if n_dom % k == 0 and k * k <= n_dom)
-    long_side = n_dom // side
+    long_side = long_side_of(n_dom)
+    side = n_dom // long_side
 
     root = (sub == 0) & (dom == 0)
     has_below, has_above = sub > 0, sub < n_sub - 1
@@ -65,17 +68,18 @@
     p_copies = [
         pltpu.make_async_copy(
             p_hbm.at[r, pl.ds(h * half, half)], p_buf.at[r, pl.ds(h * half, half)],
-            p_sem.at[2 * r + h],
+            p_sem,
         )
         for r in range(rows)
         for h in range(2)
     ]
+    p_whole = pltpu.make_async_copy(p_hbm, p_buf, p_sem)
     for copy in p_copies:
         copy.start()
     cols_copy = pltpu.make_async_copy(cols_hbm, cols, cols_sem)
     cols_copy.start()
     a_copies = [
-        pltpu.make_async_copy(a_hbm.at[r], a_buf.at[r], a_sem.at[r]) for r in range(rows)
+        pltpu.make_async_copy(a_hbm.at[r], a_buf.at[r], a_sem) for r in range(rows)
     ]
 
     @pl.when(jnp.logical_not(root))
@@ -107,10 +111,20 @@
         row = jnp.clip(send_rows[peer_at(offset, 1)], 0, rows - 1)
         stage[offset] = p_buf[row]
 
+    def arrival(offset):
+        return jnp.where(root, long_side, offset // side)
+
+    def wait_arrivals(group, number):
+        pltpu.make_async_remote_copy(
+            src_ref=stage.at[pl.ds(0, number)], dst_ref=far.at[pl.ds(0, number)],
+            send_sem=far_send.at[0], recv_sem=far_recv.at[group],
+            device_id={"dom": peer_at(1, 1)}, device_id_type=MESH,
+        ).wait_recv()
+
     def far_copy(offset, sender=0):
         return pltpu.make_async_remote_copy(
             src_ref=stage.at[offset], dst_ref=far.at[offset],
-            send_sem=far_send.at[sender], recv_sem=far_recv.at[offset],
+            send_sem=far_send.at[sender], recv_sem=far_recv.at[arrival(offset)],
             device_id={"dom": peer_at(offset, 1)}, device_id_type=MESH,
         )
 
@@ -134,9 +148,8 @@
             pl.semaphore_signal(root_in, inc=1, device_id={"dom": step}, device_id_type=MESH)
         pl.semaphore_signal(root_in, inc=1, device_id={"sub": 1}, device_id_type=MESH)
         send_rows_copy.wait()
-        for copy in p_copies:
-            copy.wait()
-        for offset in near_first(long_side, side):
+        p_whole.wait()
+        for offset in root_order(long_side, side):
             put_on_stage(offset)
             far_copy(offset).start()
         near_copy(0).start()
@@ -148,8 +161,7 @@
         for copy in a_copies:
             copy.start()
         send_rows_copy.wait()
-        for copy in p_copies:
-            copy.wait()
+        p_whole.wait()
 
         @pl.loop(1, n_dom)
         def _(offset):
@@ -193,9 +205,10 @@
     link_copy = pltpu.make_async_copy(table, links, link_sem)
     link_copy.start()
 
+    pltpu.make_async_copy(a_hbm, a_buf, a_sem).wait()
+
     for r in range(rows):
         left = p_buf[r].T
-        a_copies[r].wait()
         group = next(g for g in (9, 8, 6, 5, 4, 3, 2, 1) if per_row % g == 0)
 
         @pl.loop(0, per_row // group)
@@ -237,7 +250,6 @@
         put(n_dom + place, window(2 * rows * place, [near[place, r] for r in range(rows)]))
 
     def take_far(offset):
-        far_copy(offset).wait_recv()
         source = peer_at(offset, -1)
         put(source, window(3 * rows + source, [far[offset]]))
 
@@ -289,6 +301,15 @@
         def _():
             pl.semaphore_wait(root_in, 1)
             far_copy(back, 1).start()
+            wait_arrivals(long_side, 1)
+
+        group = offset_at(i) // side
+        number = side - count(group == 0) - count(root_far & (dom // side == group))
+        for some in range(max(1, side - 2), side + 1):
+
+            @pl.when((i % side == 0) & (number == some))
+            def _():
+                wait_arrivals(group, some)
 
         @pl.when(jnp.where(last_turn, root_far, jnp.logical_not(from_root(offset))))
         def _():
@@ -331,8 +352,8 @@
             pltpu.VMEM((3 * rows + n_dom, size, 2 * size), BF16),
             pltpu.VMEM((table_rows, 128), jnp.int32),
             pltpu.SMEM((table_rows, 128), jnp.int32),
-            dma, dma, dma((rows,)), dma((2 * rows,)), dma,
-            dma((2,)), dma((n_dom,)), dma((2,)), dma((2,)), pltpu.SemaphoreType.REGULAR,
+            dma, dma, dma, dma, dma,
+            dma((2,)), dma((long_side_of(n_dom) + 1,)), dma((2,)), dma((2,)), pltpu.SemaphoreType.REGULAR,
         ],
         compiler_params=pltpu.CompilerParams(
             collective_id=0, has_side_effects=True, vmem_limit_bytes=48 * 1024 * 1024

time: 20.3 us -> 20.1 us (level)
  the two profiles are of different devices: /device:TPU:20 before, /device:TPU:28 now
where the time goes in v5:
time: 20.1 us; the launch traced here: 19.8 us
  Pallas kernels  19 us (95%)
  local copies, waits for them, and re-layouts  0.82 us (4%)
    pallas_call x1, Pallas kernels, per_device(): pl.pallas_call(functools.partial(kernel, n_sub, n_dom, rows, per_row, siz...  19 us
    unnamed x1, local copies, waits for them, and re-layouts  0.82 us

profile of v5, /device:TPU:28, one launch (start us, length us, event | category | flops | bytes accessed | tf_op | source)
XLA Modules:
  0.0 19.8 jit_solution(7644695549807684102)
XLA Ops:
  0.0 19.0 %shard_map.46 = bf16[1,128,2304]{2,1,0:T(8,128)(2,1)S(1)} custom-call(s32[3,27]{1,0:T(4,128)} %cols_hbm.1, s32[16]{0:T(128)} %bitcast.1, bf16[3,27,128,128]{3,2,1,0:T(8,128)(2,1)} %a_hbm.1, bf16[3,128,128]{2,1,0:T(8,128)(2,1)} %p_hbm.1), custom_call_target="tpu_custom_call" | custom-call | flops 549453824 | bytes 3342336 | tf_op jit(solution)/shard_map/pallas_call | solution.py:338
  19.0 0.8 %copy.6 = bf16[1,128,2304]{2,1,0:T(8,128)(2,1)} copy(bf16[1,128,2304]{2,1,0:T(8,128)(2,1)S(1)} %shard_map.46) | data formatting | bytes 1179648

commit v6 on v5

--- a/solution.py
+++ b/solution.py
@@ -64,14 +64,14 @@
 
     send_rows_copy = pltpu.make_async_copy(send_hbm, send_rows, send_rows_sem)
     send_rows_copy.start()
-    half = size // 2
+    piece = size // 4
     p_copies = [
         pltpu.make_async_copy(
-            p_hbm.at[r, pl.ds(h * half, half)], p_buf.at[r, pl.ds(h * half, half)],
+            p_hbm.at[r, pl.ds(h * piece, piece)], p_buf.at[r, pl.ds(h * piece, piece)],
             p_sem,
         )
         for r in range(rows)
-        for h in range(2)
+        for h in range(size // piece)
     ]
     p_whole = pltpu.make_async_copy(p_hbm, p_buf, p_sem)
     for copy in p_copies:

time: 20.1 us -> 20.1 us (level)
  no operation moved by 1% of the time
where the time goes in v6:
time: 20.1 us; the launch traced here: 19.9 us
  Pallas kernels  19 us (95%)
  local copies, waits for them, and re-layouts  0.82 us (4%)
    pallas_call x1, Pallas kernels, per_device(): pl.pallas_call(functools.partial(kernel, n_sub, n_dom, rows, per_row, siz...  19 us
    unnamed x1, local copies, waits for them, and re-layouts  0.82 us

profile of v6, /device:TPU:28, one launch (start us, length us, event | category | flops | bytes accessed | tf_op | source)
XLA Modules:
  0.0 19.9 jit_solution(2757236601268108433)
XLA Ops:
  0.0 19.0 %shard_map.46 = bf16[1,128,2304]{2,1,0:T(8,128)(2,1)S(1)} custom-call(s32[3,27]{1,0:T(4,128)} %cols_hbm.1, s32[16]{0:T(128)} %bitcast.1, bf16[3,27,128,128]{3,2,1,0:T(8,128)(2,1)} %a_hbm.1, bf16[3,128,128]{2,1,0:T(8,128)(2,1)} %p_hbm.1), custom_call_target="tpu_custom_call" | custom-call | flops 549453824 | bytes 3342336 | tf_op jit(solution)/shard_map/pallas_call | solution.py:338
  19.0 0.8 %copy.6 = bf16[1,128,2304]{2,1,0:T(8,128)(2,1)} copy(bf16[1,128,2304]{2,1,0:T(8,128)(2,1)S(1)} %shard_map.46) | data formatting | bytes 1179648
